TPU v7x, 1024 devices: a whole 8x8x8 slice. The times are simulated.
1024 devices in a mesh: expert: 16 (over x_hi, z), replica: 64 (over y, x_lo, core).
Axes of the slice: x: 8 (x_hi: 2, x_lo: 4; x = x_hi * 4 + x_lo), y: 8, z: 8, core: 2. Of those that a mesh axis runs over, the one named last changes fastest.
Arguments:
- tokens: bfloat16 [4096, 1280], P(('replica', 'expert')), may hold values from -6 to 6
- upstream: bfloat16 [4096, 1280], P(('replica', 'expert')), may hold values from -6 to 6
- experts: int32 [4096, 2], P('replica'), may hold values from 0 to 15, all different within a row; in each aligned block of 64 rows (0 to 63, 64 to 127, ...) at most 10 rows name the same one
- gates: float32 [4096, 2], P('replica'), may hold values from 0.1 to 1
- w_in: bfloat16 [16, 1280, 5120], P('expert', None, 'replica'), may hold values from -0.15625 to 0.15625
- w_out: bfloat16 [16, 5120, 1280], P('expert', 'replica'), may hold values from -0.078125 to 0.078125
Outputs:
- token_grads: bfloat16 [4096, 1280], P(('replica', 'expert'))
- grad_in: float32 [16, 1280, 5120], P('expert', None, 'replica')
- grad_out: float32 [16, 5120, 1280], P('expert', 'replica')
Inputs may be any that keep to these rules, and one draw needn't show every extreme that they name: The two experts of a token differ. Among the 64 tokens of one group no expert is named more than 10 times, a bound that some block reaches; every expert is named somewhere.
All inputs are finite; a program needn't handle non-finite values.
Results may differ from a plain program's by a relative error of at most 0.0057.
Values may be sent and summed in bfloat16 or wider, within the bound.
A program may use at most 32 MiB of HBM per device.

v0:
```python
import jax
import jax.numpy as jnp
from jax import lax
from jax.sharding import PartitionSpec as P


def contract_last(left, right):
    return lax.dot_general(
        left, right, (((1,), (1,)), ((), ())), preferred_element_type=jnp.float32
    )


def contract_first(left, right):
    return lax.dot_general(
        left, right, (((0,), (0,)), ((), ())), preferred_element_type=jnp.float32
    )


def local(tokens, upstream, experts, gates, w_in, w_out):
    row_x, row_dy = (
        lax.all_gather(tokens, "expert", axis=0, tiled=True),
        lax.all_gather(upstream, "expert", axis=0, tiled=True),
    )
    own_expert = lax.axis_index("expert")
    n_expert = lax.axis_size("expert")
    tok_dev = tokens.shape[0]
    count_row = row_x.shape[0]
    width = row_x.shape[1]
    slots = 5 * tok_dev // 2
    flat_ids = experts.reshape(-1)
    onehot = (flat_ids[:, None] == jnp.arange(n_expert, dtype=jnp.int32)[None, :]).astype(jnp.int32)
    before = jnp.cumsum(onehot, axis=0) - onehot
    slot_pos = jnp.sum(before * onehot, axis=1)
    chosen = (flat_ids == own_expert)[None, :] & (
        slot_pos[None, :] == jnp.arange(slots, dtype=jnp.int32)[:, None]
    )
    chosen = chosen.reshape(slots, count_row, 2)
    pick = jnp.any(chosen, axis=2).astype(jnp.bfloat16)
    slot_gate = jnp.sum(jnp.where(chosen, gates[None, :, :], 0.0), axis=(1, 2))
    slot_in = jnp.dot(pick, row_x, preferred_element_type=jnp.float32).astype(jnp.bfloat16)
    slot_dy = jnp.dot(pick, row_dy, preferred_element_type=jnp.float32)
    slot_grad = (slot_gate[:, None] * slot_dy).astype(jnp.bfloat16)
    weight_in = w_in[0]
    weight_out = w_out[0]
    kept_rows = 1
    x_all = jnp.zeros((kept_rows, width), jnp.bfloat16)
    part_x = lax.all_gather(slot_in, "replica", axis=0, tiled=True)
    part_g = lax.all_gather(slot_grad, "replica", axis=0, tiled=True)
    pre = jnp.dot(part_x, weight_in, preferred_element_type=jnp.float32)
    act, back = jax.vjp(jax.nn.gelu, pre)
    dh = contract_last(part_g, weight_out)
    dpre = back(dh)[0].astype(jnp.bfloat16)
    acc_out = contract_first(act.astype(jnp.bfloat16), part_g)
    acc_in = contract_first(part_x, dpre)
    acc_in, acc_out, dpre_all, x_all = (acc_in, acc_out, dpre, x_all)
    slot_dx = lax.psum_scatter(
        contract_last(dpre_all, weight_in), "replica", scatter_dimension=0, tiled=True
    )
    every_slot = lax.all_gather(slot_dx, "expert", axis=0, tiled=True)
    address = (flat_ids * slots + slot_pos).reshape(count_row, 2)
    own_address = lax.dynamic_slice_in_dim(address, own_expert * tok_dev, tok_dev, 0)
    hits = jnp.sum(
        (
            own_address[:, :, None] == jnp.arange(n_expert * slots, dtype=jnp.int32)[None, None, :]
        ).astype(jnp.float32),
        axis=1,
    )
    token_grad = jnp.dot(
        hits, every_slot, precision=lax.Precision.HIGHEST, preferred_element_type=jnp.float32
    )
    return (token_grad.astype(jnp.bfloat16), acc_in[None], acc_out[None])


def solution(mesh):
    in_specs = (
        P(("replica", "expert"), None),
        P(("replica", "expert"), None),
        P("replica", None),
        P("replica", None),
        P("expert", None, "replica"),
        P("expert", "replica", None),
    )
    out_specs = (
        P(("replica", "expert"), None),
        P("expert", None, "replica"),
        P("expert", "replica", None),
    )
    return jax.shard_map(local, mesh=mesh, in_specs=in_specs, out_specs=out_specs, check_vma=False)
```

profile of v0, /device:TPU:1, one launch (start us, length us, event | category | flops | bytes accessed | tf_op | source)
XLA Modules:
  0.0 937.1 jit_solution(15252744292166925002)
XLA Ops:
  7.2 0.8 copy.30
  8.0 0.7 broadcast_compare_fusion
  8.9 0.2 reduce_window_sum.11
  9.1 0.2 select_reduce_fusion
  9.3 0.1 reduce_sum.30
  9.5 60.3 %all-gather.2 = bf16[16,4,1280]{2,1,0:T(4,128)(2,1)S(1)} all-gather(bf16[1,4,1280]{2,1,0:T(4,128)(2,1)} %bitcast.35), channel_id=1, replica_groups=mesh['expert'=16,'replica'=64] {'expert'}, dimensions={0}, use_global_device_ids=true | all-gather | bytes 174080 | tf_op jit(solution)/shard_map/all_gather | solution.py:21
  69.8 0.8 fusion.1
  70.7 40.4 %all-gather = bf16[16,4,1280]{2,1,0:T(4,128)(2,1)S(1)} all-gather(bf16[1,4,1280]{2,1,0:T(4,128)(2,1)} %bitcast.36), channel_id=1, replica_groups=mesh['expert'=16,'replica'=64] {'expert'}, dimensions={0}, use_global_device_ids=true | all-gather | bytes 174080 | tf_op jit(solution)/shard_map/all_gather | solution.py:22
  111.3 0.8 fusion.2
  112.1 78.4 %all-gather.10.cloned.1.call-done = bf16[64,10,1280]{2,1,0:T(8,128)(2,1)} async-done(((bf16[1,10,1280]{2,1,0:T(8,128)(2,1)}), bf16[64,10,1280]{2,1,0:T(8,128)(2,1)}) %all-gather.10.cloned.1.call-update) | async-done | bytes 1638416 | tf_op jit(solution)/shard_map/all_gather | solution.py:47
  190.5 2.7 reshape.39
  193.3 1.3 fusion.12
  194.6 119.5 %all-gather.8.cloned.1.call-done = bf16[64,10,1280]{2,1,0:T(8,128)(2,1)} async-done(((bf16[1,10,1280]{2,1,0:T(8,128)(2,1)}), bf16[64,10,1280]{2,1,0:T(8,128)(2,1)}) %all-gather.8.cloned.1.call-update) | async-done | bytes 1638416 | tf_op jit(solution)/shard_map/all_gather | solution.py:48
  314.0 2.7 reshape.35
  316.8 1.7 fusion.9
  318.5 0.6 copy-done.2
  319.1 2.3 fusion.10
  321.5 1.3 dynamic-slice
  323.6 2.0 convolution_bitcast_fusion
  325.6 1.2 convolution_bitcast_fusion.1
  326.8 542.5 %all-reduce.3.cloned.1.call-done = f32[640,1280]{1,0:T(8,128)} async-done(((f32[640,1280]{1,0:T(8,128)}), f32[640,1280]{1,0:T(8,128)}) %all-reduce.3.cloned.1.call-update) | async-done | bytes 3276816
  869.3 0.9 dynamic-slice_bitcast_fusion
  870.2 59.2 %all-gather.4 = f32[16,10,1280]{2,1,0:T(8,128)S(1)} all-gather(f32[1,10,1280]{2,1,0:T(8,128)S(1)} %dynamic-slice_bitcast_fusion), channel_id=1, replica_groups=mesh['expert'=16,'replica'=64] {'expert'}, dimensions={0}, use_global_device_ids=true | all-gather | bytes 870400 | tf_op jit(solution)/shard_map/all_gather | solution.py:59
  929.5 1.1 convolution_convert_fusion.1
  (26 shorter events, 1.0 us)
Async XLA Ops:
  7.2 186.1 %copy-start = (bf16[1,1280,80]{1,2,0:T(8,128)(2,1)S(1)}, bf16[1,1280,80]{1,2,0:T(8,128)(2,1)}, u32[]{:S(2)}) copy-start(bf16[1,1280,80]{1,2,0:T(8,128)(2,1)} %param.10) | copy-start | bytes 614404
  7.2 104.0 %copy-start.4 = (f32[64,2]{0,1:T(2,128)S(1)}, f32[64,2]{0,1:T(2,128)}, u32[]{:S(2)}) copy-start(f32[64,2]{0,1:T(2,128)} %param.9) | copy-start | bytes 1540
  7.2 183.3 %all-gather.10.cloned.1.call-start = ((), (), s32[]{:S(2)}) async-start(), calls=%async_computation.1 | async-start | bytes 2662400 | tf_op jit(solution)/shard_map/all_gather | solution.py:47
  70.6 243.4 %all-gather.8.cloned.1.call-start = ((), (), s32[]{:S(2)}) async-start(), calls=%async_computation | async-start | bytes 2662400 | tf_op jit(solution)/shard_map/all_gather | solution.py:48
  112.1 757.2 %all-reduce.3.cloned.1.call-start = ((), (), s32[]{:S(2)}) async-start(), calls=%async_computation.2 | async-start | bytes 6553600
  318.5 0.6 copy-start.2
  321.4 2.0 copy-start.3
  323.4 2.2 copy-start.1
Sparse Core Ops, SparseCore 0:
  70.7 119.7 all-gather.9
  193.8 120.1 all-gather.7
  321.6 547.6 all-reduce.2
where the time goes:
time: 942 us; the launch traced here: 937 us
  waiting for transfers between devices  740 us (79%)
  blocking collectives  160 us (17%)
  between operations  14.5 us (2%)
  matrix products  11.1 us (1%)
  local copies, waits for them, and re-layouts  9.68 us (1%)
    unnamed x4, waiting for transfers between devices  543 us
    all_gather x1, waiting for transfers between devices, local(): part_g = lax.all_gather(slot_grad, 'replica', axis=0, tiled=True)  119 us
    all_gather x1, waiting for transfers between devices, local(): part_x = lax.all_gather(slot_in, 'replica', axis=0, tiled=True)  78.4 us
    all_gather x1, blocking collectives, local(): lax.all_gather(tokens, 'expert', axis=0, tiled=True)  60.3 us
    all_gather x1, blocking collectives, local(): every_slot = lax.all_gather(slot_dx, 'expert', axis=0, tiled=True)  59.2 us
    all_gather x1, blocking collectives, local(): lax.all_gather(upstream, 'expert', axis=0, tiled=True)  40.4 us
  transfers between devices with their start and end apart: 3, of which 3 were waited for; matrix products, arithmetic and copies ran while one was open for 1% of the time, Pallas kernels for 0%

commit v1 on v0

v1 whole, which is shorter than its diff:
```python
import functools

import jax
import jax.numpy as jnp
from jax import lax
from jax.experimental import pallas as pl
from jax.experimental.pallas import tpu as pltpu
from jax.sharding import PartitionSpec as P

MESH = pl.DeviceIdType.MESH
F32 = jnp.float32
BF16 = jnp.bfloat16
NZ, NH, NY, NX = 8, 2, 8, 4
NE = NZ * NH
SLOTS = 10
HALF = 640
GRP = NX * SLOTS
PLACE = {4: 0, 3: 1, 5: 2, 2: 3, 6: 4, 1: 5, 7: 6, 0: 7}


def iota(shape, dim):
    return lax.broadcasted_iota(jnp.int32, shape, dim)


def onehot(mask):
    return mask.astype(F32).astype(BF16)


def dot(a, b, dims=((1,), (0,))):
    return lax.dot_general(a, b, (dims, ((), ())), preferred_element_type=F32)


def tens(c):
    return (
        (c >= 10).astype(jnp.int32)
        + (c >= 20).astype(jnp.int32)
        + (c >= 30).astype(jnp.int32)
    )


def kernel(
    tok, up, ids, gates, w1, w2,
    out_tok, out_in, out_out,
    abuf, bbuf, X, G, W1, W2, dx, csend, crecv, vcat, psend, precv,
    dsend, drecv, gsend, grecv,
    a_send, a_recv, w_send, w_recv, b_send, b_recv, c_send, c_recv,
    p_send, p_recv, d_send, d_recv, g_send, g_recv,
):
    e = lax.axis_index("expert")
    r = lax.axis_index("replica")
    xh, z = e // NZ, e % NZ
    y, x, core = r // (NX * 2), (r // 2) % NX, r % 2

    def to_expert(e2):
        return {"expert": e2, "replica": r}

    def to_replica(y2, x2, c2):
        return {"expert": e, "replica": (y2 * NX + x2) * 2 + c2}

    twin = to_replica(y, x, 1 - core)
    y_up = to_replica((y + 1) % NY, x, core)
    y_dn = to_replica((y + NY - 1) % NY, x, core)
    x_peer = [None] + [to_replica(y, (x + d) % NX, core) for d in range(1, NX)]
    e_peer = [None] + [to_expert((e + d) % NE) for d in range(1, NE)]
    z_peer = [None] + [to_expert(xh * NZ + (z + d) % NZ) for d in range(1, NZ)]
    mirror = to_expert((1 - xh) * NZ + z)

    barrier = pltpu.get_barrier_semaphore()
    peers = [twin, y_up, y_dn] + x_peer[1:] + e_peer[1:]
    for peer in peers:
        pl.semaphore_signal(barrier, inc=1, device_id=peer, device_id_type=MESH)

    started = []

    def send(src, dst, s_sem, r_sem, peer):
        copy = pltpu.make_async_remote_copy(
            src_ref=src, dst_ref=dst, send_sem=s_sem, recv_sem=r_sem,
            device_id=peer, device_id_type=MESH,
        )
        copy.start()
        started.append(copy)

    def arrived(dst, r_sem, s_sem, peer):
        pltpu.make_async_remote_copy(
            src_ref=dst, dst_ref=dst, send_sem=s_sem, recv_sem=r_sem,
            device_id=peer, device_id_type=MESH,
        ).wait_recv()

    abuf[e] = jnp.concatenate(
        [
            tok[:, :HALF].astype(F32), tok[:, HALF:].astype(F32),
            up[:, :HALF].astype(F32), up[:, HALF:].astype(F32),
        ],
        axis=0,
    ).astype(BF16)
    W1[0:80] = w1[...]
    W2[0:80] = w2[...]
    pl.semaphore_wait(barrier, len(peers))

    own = abuf.at[e]
    send(own, own, a_send.at[0], a_recv.at[e], mirror)
    for d in (4, 3, 5, 2, 6, 1, 7):
        send(own, own, a_send.at[d], a_recv.at[e], z_peer[d])
    send(w1, W1.at[pl.ds(80, 80)], w_send.at[0], w_recv.at[0], twin)
    send(w2, W2.at[pl.ds(80, 80)], w_send.at[1], w_recv.at[1], twin)

    id0, id1 = ids[0:1, :], ids[1:2, :]
    hit0, hit1 = id0 == e, id1 == e
    chosen = (hit0 | hit1).astype(F32)
    gate = jnp.where(hit0, gates[0:1, :], jnp.where(hit1, gates[1:2, :], 0.0))
    ch8 = jnp.broadcast_to(chosen, (8, 64))
    tri = onehot(iota((64, 64), 0) < iota((64, 64), 1))
    v8 = jnp.where(ch8 > 0.5, dot(ch8.astype(BF16), tri), 99.0)
    c256 = iota((64, 256), 1)
    spread = onehot(iota((64, 256), 0) == (c256 >> 4) * 4 + (c256 & 3))
    vexp = dot(v8.astype(BF16), spread)[0:1, :]
    r40 = iota((GRP, 256), 0)
    part = tens(r40)
    slot = (r40 - 10 * part).astype(F32)
    col = iota((GRP, 256), 1)
    pick = onehot((vexp == slot) & (part == ((col >> 2) & 3)))
    slot64 = slot[:, 0:64]
    gcol = jnp.sum(jnp.where(v8[0:1, :] == slot64, gate, 0.0), axis=1, keepdims=True)
    gcol = jnp.where(part[:, 0:1] >= 2, gcol, 1.0)

    pe = (1 - xh) * NZ + z
    arrived(abuf.at[pe], a_recv.at[pe], a_send.at[0], mirror)
    for d in (4, 3, 5, 2, 6, 1, 7):
        send(abuf.at[pe], abuf.at[pe], a_send.at[NZ + d], a_recv.at[pe], z_peer[d])
    for h in range(2):
        for d in range(1, NZ):
            s = ((xh + h) % 2) * NZ + (z + d) % NZ
            arrived(abuf.at[s], a_recv.at[s], a_send.at[0], z_peer[d])
    rows = abuf[...].reshape(NE * 16, HALF)
    bbuf[y, x] = (dot(pick, rows) * gcol).astype(BF16)

    p160, c160 = iota((4 * GRP, GRP), 0), iota((4 * GRP, GRP), 1)
    perms = [onehot(p160 == c160 + 30 * tens(c160) + 10 * j) for j in range(NX)]

    def assemble(d):
        yy = (y + d) % NY
        m = dot(perms[0], bbuf[yy, 0])
        for j in range(1, NX):
            m = m + dot(perms[j], bbuf[yy, j])
        m = m.astype(BF16)
        at = PLACE[d] * GRP
        X[at:at + GRP, 0:HALF] = m[0:GRP]
        X[at:at + GRP, HALF:] = m[GRP:2 * GRP]
        G[at:at + GRP, 0:HALF] = m[2 * GRP:3 * GRP]
        G[at:at + GRP, HALF:] = m[3 * GRP:4 * GRP]

    mine = bbuf.at[y, x]
    b_at = [0]

    def b_go(yy, j, peer):
        ref = bbuf.at[yy, j]
        send(ref, ref, b_send.at[b_at[0]], b_recv.at[yy * NX + j], peer)
        b_at[0] += 1

    def b_in(yy, j, peer):
        arrived(bbuf.at[yy, j], b_recv.at[yy * NX + j], b_send.at[0], peer)

    b_go(y, x, y_up)
    b_go(y, x, y_dn)
    for d in (2, 1, 3):
        b_go(y, x, x_peer[d])
    for k in range(0, 5):
        for c in range(NX):
            j = (x + c) % NX
            n_up = 4 if c % 2 == 0 else 3
            n_dn = 7 - n_up
            if k == 0:
                if c > 0:
                    b_in(y, j, x_peer[c])
                    b_go(y, j, y_up)
                    b_go(y, j, y_dn)
                continue
            if k <= n_up:
                yy = (y + NY - k) % NY
                b_in(yy, j, y_dn)
                if k < n_up:
                    b_go(yy, j, y_up)
            if k <= n_dn:
                yy = (y + k) % NY
                b_in(yy, j, y_up)
                if k < n_dn:
                    b_go(yy, j, y_dn)
        assemble(k % NY)
        if 0 < k < 4:
            assemble(NY - k)

    arrived(W1.at[pl.ds(80, 80)], w_recv.at[0], w_send.at[0], twin)
    arrived(W2.at[pl.ds(80, 80)], w_recv.at[1], w_send.at[1], twin)

    last = ((1,), (1,))
    pre = dot(W1[...], X[...], last)
    dh = dot(W2[...], G[...], last)
    k0 = 0.7978845608028654
    sq = pre * pre
    t = jnp.tanh(k0 * (pre + 0.044715 * (sq * pre)))
    cdf = 0.5 * (1.0 + t)
    act = (pre * cdf).astype(BF16)
    slope = cdf + pre * (0.5 * (1.0 - t * t)) * (k0 * (1.0 + 3 * 0.044715 * sq))
    dpre32 = dh * slope
    dpre = dpre32.astype(BF16)
    dx[...] = dot(dpre32.T.astype(BF16), W1[...])

    def c_index(c, sign, k):
        return c * 7 + k + (0 if sign > 0 else (4 if c == 0 else 3))

    def c_step(k):
        for c in range(2):
            for sign in (1, -1):
                n = 4 if (c == 0) == (sign > 0) else 3
                if k >= n:
                    continue
                d = sign * (n - k)
                at = PLACE[d % NY] * GRP
                val = dx[at:at + GRP, c * HALF:(c + 1) * HALF]
                if k > 0:
                    i = c_index(c, sign, k - 1)
                    arrived(crecv.at[i], c_recv.at[i], c_send.at[i], y_dn if sign > 0 else y_up)
                    val = val + crecv[i].astype(F32)
                i = c_index(c, sign, k)
                csend[i] = val.astype(BF16)
                send(csend.at[i], crecv.at[i], c_send.at[i], c_recv.at[i], y_up if sign > 0 else y_dn)

    c_step(0)
    g_in = dot(dpre, X[...])
    out_in[...] = g_in[0:80]
    gsend[0] = g_in[80:160]
    send(gsend.at[0], grecv.at[0], g_send.at[0], g_recv.at[0], twin)
    c_step(1)
    g_out = dot(act, G[...])
    out_out[...] = g_out[0:80]
    gsend[1] = g_out[80:160]
    send(gsend.at[1], grecv.at[1], g_send.at[1], g_recv.at[1], twin)
    c_step(2)
    c_step(3)
    for c in range(2):
        at = PLACE[0] * GRP
        val = dx[at:at + GRP, c * HALF:(c + 1) * HALF]
        for sign in (1, -1):
            n = 4 if (c == 0) == (sign > 0) else 3
            i = c_index(c, sign, n - 1)
            arrived(crecv.at[i], c_recv.at[i], c_send.at[i], y_dn if sign > 0 else y_up)
            val = val + crecv[i].astype(F32)
        vcat[c * GRP:(c + 1) * GRP] = val.astype(BF16)

    q_row, q_col = iota((24, 2 * GRP), 0), iota((24, 2 * GRP), 1)
    q_half = (q_row >= 10).astype(jnp.int32)
    q_at = jnp.where(q_row < 20, q_half * 30 + q_row, -1000)
    sums = vcat[...]
    for d in (2, 1, 3):
        j = (x + d) % NX
        psend[d - 1] = dot(onehot(q_col == q_at + 10 * j), sums).astype(BF16)
        send(psend.at[d - 1], precv.at[d - 1], p_send.at[d - 1], p_recv.at[d - 1], x_peer[d])
    total = dot(onehot(q_col == q_at + 10 * x), sums)

    r64 = iota((128, 64), 0)
    gather = onehot(iota((128, 64), 1) == (r64 >> 3) * 4 + (r64 & 3))
    v_row = dot(gather, v8.astype(BF16), last)[:, 0:1]
    t_row, t_col = iota((128, 24), 0), iota((128, 24), 1)
    t_half = (t_col >= 10).astype(jnp.int32)
    t_slot = jnp.where(t_col < 20, t_col - 10 * t_half, 50).astype(F32)
    back = onehot((v_row == t_slot) & (((t_row >> 2) & 1) == t_half))

    for d in (1, 3, 2):
        arrived(precv.at[d - 1], p_recv.at[d - 1], p_send.at[d - 1], x_peer[NX - d])
        total = total + precv[d - 1].astype(F32)
    spread_rows = dot(back, total.astype(BF16))
    dsend[...] = spread_rows.reshape(NE, 8, HALF).astype(BF16)
    for d in (8, 12, 4, 9, 7, 10, 6, 11, 5, 13, 3, 14, 2, 15, 1):
        send(dsend.at[(e + d) % NE], drecv.at[d - 1], d_send.at[d - 1], d_recv.at[d - 1], e_peer[d])

    for i, out in ((0, out_in), (1, out_out)):
        arrived(grecv.at[i], g_recv.at[i], g_send.at[i], twin)
        out[...] = out[...] + grecv[i]

    res = dsend[e].astype(F32)
    for d in range(1, NE):
        arrived(drecv.at[d - 1], d_recv.at[d - 1], d_send.at[d - 1], e_peer[NE - d])
        res = res + drecv[d - 1].astype(F32)
    out_tok[:, :HALF] = res[0:4].astype(BF16)
    out_tok[:, HALF:] = res[4:8].astype(BF16)

    for copy in started:
        copy.wait_send()


def local(tokens, upstream, experts, gates, w_in, w_out):
    vmem = pl.BlockSpec(memory_space=pltpu.VMEM)
    dma = pltpu.SemaphoreType.DMA
    rows = NY * GRP
    width = 2 * HALF
    out_tok, out_in, out_out = pl.pallas_call(
        kernel,
        out_shape=(
            jax.ShapeDtypeStruct((4, width), BF16),
            jax.ShapeDtypeStruct((80, width), F32),
            jax.ShapeDtypeStruct((80, width), F32),
        ),
        in_specs=[vmem] * 6,
        out_specs=(vmem, vmem, vmem),
        scratch_shapes=[
            pltpu.VMEM((NE, 16, HALF), BF16),
            pltpu.VMEM((NY, NX, GRP, HALF), BF16),
            pltpu.VMEM((rows, width), BF16),
            pltpu.VMEM((rows, width), BF16),
            pltpu.VMEM((160, width), BF16),
            pltpu.VMEM((160, width), BF16),
            pltpu.VMEM((rows, width), F32),
            pltpu.VMEM((14, GRP, HALF), BF16),
            pltpu.VMEM((14, GRP, HALF), BF16),
            pltpu.VMEM((2 * GRP, HALF), BF16),
            pltpu.VMEM((3, 24, HALF), BF16),
            pltpu.VMEM((3, 24, HALF), BF16),
            pltpu.VMEM((NE, 8, HALF), BF16),
            pltpu.VMEM((NE - 1, 8, HALF), BF16),
            pltpu.VMEM((2, 80, width), F32),
            pltpu.VMEM((2, 80, width), F32),
            dma((NE,)), dma((NE,)), dma((2,)), dma((2,)), dma((31,)), dma((32,)),
            dma((14,)), dma((14,)), dma((3,)), dma((3,)), dma((15,)), dma((15,)),
            dma((2,)), dma((2,)),
        ],
        compiler_params=pltpu.CompilerParams(
            collective_id=0, has_side_effects=True, vmem_limit_bytes=40 * 1024 * 1024
        ),
        cost_estimate=pl.CostEstimate(flops=700_000_000, bytes_accessed=2_000_000, transcendentals=51200),
        name="moe_backward",
    )(tokens, upstream, experts.T, gates.T, w_in[0].T, w_out[0])
    return out_tok, out_in.T[None], out_out[None]


def solution(mesh):
    in_specs = (
        P(("replica", "expert"), None),
        P(("replica", "expert"), None),
        P("replica", None),
        P("replica", None),
        P("expert", None, "replica"),
        P("expert", "replica", None),
    )
    out_specs = (
        P(("replica", "expert"), None),
        P("expert", None, "replica"),
        P("expert", "replica", None),
    )
    return jax.shard_map(local, mesh=mesh, in_specs=in_specs, out_specs=out_specs, check_vma=False)
```

time: 942 us -> 95.9 us (0.10)
  the two profiles are of different devices: /device:TPU:1 before, /device:TPU:16 now
where the time goes in v1:
time: 95.9 us; the launch traced here: 95.6 us
  Pallas kernels  88.9 us (93%)
  local copies, waits for them, and re-layouts  6.05 us (6%)
    pallas_call x1, Pallas kernels, local(): pl.pallas_call(kernel, out_shape=(jax.ShapeDtypeStruct((4, width), BF16),...  88.9 us
    unnamed x15, local copies, waits for them, and re-layouts  6.05 us

profile of v1, /device:TPU:16, one launch (start us, length us, event | category | flops | bytes accessed | tf_op | source)
XLA Modules:
  0.0 95.6 jit_solution(8094314781340017981)
XLA Ops:
  0.6 0.0 copy-start.5
  0.6 0.0 copy-start.4
  0.7 0.7 copy-done.5
  1.3 0.0 copy-done.4
  1.3 0.0 copy-start
  1.3 0.9 copy-done
  2.3 0.0 copy-start.1
  2.3 0.9 copy-done.1
  3.2 0.0 copy-start.2
  3.2 0.7 copy-done.2
  3.9 0.0 copy-start.3
  3.9 0.7 copy-done.3
  4.6 88.9 %moe_backward.1 = (bf16[4,1280]{1,0:T(4,128)(2,1)S(1)}, f32[80,1280]{1,0:T(8,128)S(1)}, f32[80,1280]{1,0:T(8,128)S(1)}) custom-call(bf16[4,1280]{1,0:T(4,128)(2,1)S(1)} %copy-done.2, bf16[4,1280]{1,0:T(4,128)(2,1)S(1)} %copy-done.3, s32[2,64]{1,0:T(2,128)S(1)} %bitcast.14, f32[2,64]{1,0:T(2,128)S(1)} %bitcast.15, bf16[80,1280]{1,0:T(8,128)(2,1)S(1)} %bitcast.12, ...), custom_call_target="tpu_custom_call" | custom-call | flops 700000000 | bytes 2000000 | tf_op jit(solution)/shard_map/moe_backward/pallas_call | solution.py:296
  93.5 0.6 copy.12
  94.1 0.8 copy.13
  94.9 0.8 copy.14
Async XLA Ops:
  0.6 0.7 copy-start.5
  0.6 0.7 copy-start.4
  1.3 0.9 copy-start
  2.3 0.9 copy-start.1
  3.2 0.7 copy-start.2
  3.9 0.7 copy-start.3

commit v2 on v1

v2 whole, which is shorter than its diff:
```python
import functools

import jax
import jax.numpy as jnp
from jax import lax
from jax.experimental import pallas as pl
from jax.experimental.pallas import tpu as pltpu
from jax.sharding import PartitionSpec as P

MESH = pl.DeviceIdType.MESH
F32 = jnp.float32
BF16 = jnp.bfloat16
NZ, NH, NY, NX = 8, 2, 8, 4
NE = NZ * NH
HALF = 640


def iota(shape, dim):
    return lax.broadcasted_iota(jnp.int32, shape, dim)


def onehot(mask):
    return mask.astype(F32).astype(BF16)


def dot(a, b, dims=((1,), (0,))):
    return lax.dot_general(a, b, (dims, ((), ())), preferred_element_type=F32)


def kernel(
    tok_hbm, up_hbm, ids_hbm, gates_hbm, w1, w2,
    out_tok, out_in, out_out,
    tok, up, ids, gates,
    abuf, bbuf, X, G, W1, W2, dx, csend, crecv,
    dsend, drecv, gtwin, gfrom, gsend, grecv,
    load_sem, a_send, a_recv, w_send, w_recv, b_send, b_recv, c_send, c_recv,
    d_send, d_recv, t_send, t_recv, g_send, g_recv,
):
    e = lax.axis_index("expert")
    r = lax.axis_index("replica")
    xh, z = e // NZ, e % NZ
    y, x, core = r // (NX * 2), (r // 2) % NX, r % 2

    def to_expert(e2):
        return {"expert": e2, "replica": r}

    def to_replica(y2, x2, c2):
        return {"expert": e, "replica": (y2 * NX + x2) * 2 + c2}

    twin = to_replica(y, x, 1 - core)
    home = (y % 2) * 2 + x % 2
    column = [home, home + 1 - 2 * (home % 2), (home + 2) % 4, 3 - home]
    x_flip, y_flip = x + 1 - 2 * (x % 2), y + 1 - 2 * (y % 2)
    chip_peer = [None, to_replica(y, x_flip, core), to_replica(y_flip, x, core), to_replica(y_flip, x_flip, core)]
    def place(d):
        return (y + 2 * (d // 2)) % NY, (x + 2 * (d % 2)) % NX

    def number(d):
        y2, x2 = place(d)
        return (y2 // 2) * 2 + x2 // 2

    group_peer = [None] + [to_replica(*place(d), core) for d in range(1, NY)]
    seen = [0] + [((4 - d // 2) % 4) * 2 + d % 2 for d in range(1, NY)]
    this = number(0)
    e_peer = [None] + [to_expert((e + d) % NE) for d in range(1, NE)]
    z_peer = [None] + [to_expert(xh * NZ + (z + d) % NZ) for d in range(1, NZ)]
    mirror = to_expert((1 - xh) * NZ + z)
    far_first = (4, 3, 5, 2, 6, 1, 7)
    groups_first = (5, 3, 7, 4, 1, 2, 6)

    barrier = pltpu.get_barrier_semaphore()
    peers = [twin] + group_peer[1:] + chip_peer[1:] + e_peer[1:]
    for peer in peers:
        pl.semaphore_signal(barrier, inc=1, device_id=peer, device_id_type=MESH)

    me = home * 2 + core
    loads = [
        pltpu.make_async_copy(src, dst, load_sem.at[i])
        for i, (src, dst) in enumerate(
            (
                (tok_hbm, tok), (up_hbm, up), (ids_hbm, ids), (gates_hbm, gates),
                (w1, W1.at[me]), (w2, W2.at[me]),
            )
        )
    ]
    for load in loads:
        load.start()
    started = []

    def send(src, dst, s_sem, r_sem, peer):
        copy = pltpu.make_async_remote_copy(
            src_ref=src, dst_ref=dst, send_sem=s_sem, recv_sem=r_sem,
            device_id=peer, device_id_type=MESH,
        )
        copy.start()
        started.append(copy)

    def arrived(dst, r_sem, s_sem, peer):
        pltpu.make_async_remote_copy(
            src_ref=dst, dst_ref=dst, send_sem=s_sem, recv_sem=r_sem,
            device_id=peer, device_id_type=MESH,
        ).wait_recv()

    loads[0].wait()
    loads[1].wait()
    abuf[e] = jnp.concatenate(
        [
            tok[:, :HALF].astype(F32), tok[:, HALF:].astype(F32),
            up[:, :HALF].astype(F32), up[:, HALF:].astype(F32),
        ],
        axis=0,
    ).astype(BF16)
    pl.semaphore_wait(barrier, len(peers))

    own = abuf.at[e]
    send(own, own, a_send.at[0], a_recv.at[e], mirror)
    for d in far_first:
        send(own, own, a_send.at[d], a_recv.at[e], z_peer[d])
    loads[4].wait()
    loads[5].wait()
    weights = (W1, W2)

    def w_go(i, at, s_at, peer):
        ref = weights[i].at[at]
        send(ref, ref, w_send.at[i, s_at], w_recv.at[i, at], peer)

    def w_in(i, at, peer):
        arrived(weights[i].at[at], w_recv.at[i, at], w_send.at[i, 0], peer)

    w_go(0, me, 1, chip_peer[1])
    w_go(0, me, 2, chip_peer[2])
    w_go(0, me, 0, twin)
    w_go(1, me, 0, twin)

    loads[2].wait()
    loads[3].wait()
    id0, id1 = ids[0:1, :], ids[1:2, :]
    hit0, hit1 = id0 == e, id1 == e
    chosen = (hit0 | hit1).astype(F32)
    gate = jnp.where(hit0, gates[0:1, :], jnp.where(hit1, gates[1:2, :], 0.0))
    ch8 = jnp.broadcast_to(chosen, (8, 64))
    tri = onehot(iota((64, 64), 0) < iota((64, 64), 1))
    v8 = jnp.where(ch8 > 0.5, dot(ch8.astype(BF16), tri), 99.0)
    c256 = iota((64, 256), 1)
    spread = onehot(iota((64, 256), 0) == (c256 >> 4) * 4 + (c256 & 3))
    vexp = dot(v8.astype(BF16), spread)[0:1, :]
    r40 = iota((40, 256), 0)
    part = jnp.where(r40 < 32, r40 >> 3, (r40 >> 1) & 3)
    slot = jnp.where(r40 < 32, r40 & 7, 8 + (r40 & 1)).astype(F32)
    col = iota((40, 256), 1)
    pick = onehot((vexp == slot) & (part == ((col >> 2) & 3)))
    slot64 = slot[:, 0:64]
    gcol = jnp.sum(jnp.where(v8[0:1, :] == slot64, gate, 0.0), axis=1, keepdims=True)
    gcol = jnp.where(part[:, 0:1] >= 2, gcol, 1.0)

    pe = (1 - xh) * NZ + z
    arrived(abuf.at[pe], a_recv.at[pe], a_send.at[0], mirror)
    for d in far_first:
        send(abuf.at[pe], abuf.at[pe], a_send.at[NZ + d], a_recv.at[pe], z_peer[d])
    w_go(1, me, 1, chip_peer[1])
    w_go(1, me, 2, chip_peer[2])
    for h in range(2):
        for d in range(1, NZ):
            s = ((xh + h) % 2) * NZ + (z + d) % NZ
            arrived(abuf.at[s], a_recv.at[s], a_send.at[0], z_peer[d])
    rows = abuf[...].reshape(NE * 16, HALF)
    bbuf[this] = (dot(pick, rows) * gcol).astype(BF16)

    for d in groups_first:
        send(bbuf.at[this], bbuf.at[this], b_send.at[d], b_recv.at[this], group_peer[d])

    ats = [column[c] * 2 + core for c in range(4)]
    w_in(0, ats[1], chip_peer[1])
    w_go(0, ats[1], 3, chip_peer[2])
    w_in(1, ats[2], chip_peer[2])
    w_go(1, ats[2], 3, chip_peer[1])
    w_go(0, ats[1], 4, twin)
    w_go(1, ats[2], 4, twin)
    w_in(0, ats[2], chip_peer[2])
    w_go(0, ats[2], 5, twin)
    w_in(1, ats[1], chip_peer[1])
    w_go(1, ats[1], 5, twin)
    w_in(0, ats[3], chip_peer[2])
    w_go(0, ats[3], 6, twin)
    w_in(1, ats[3], chip_peer[1])
    w_go(1, ats[3], 6, twin)

    for d in range(1, NY):
        yy = number(d)
        arrived(bbuf.at[yy], b_recv.at[yy], b_send.at[0], group_peer[d])
    for yy in range(NY):
        for k, (out, lane) in enumerate(((X, 0), (X, HALF), (G, 0), (G, HALF))):
            out[yy * 8:yy * 8 + 8, lane:lane + HALF] = bbuf[yy, 8 * k:8 * k + 8]
    tails = jnp.concatenate([bbuf[yy, 32:40] for yy in range(NY)], axis=0)
    o64, i64 = iota((64, 64), 0), iota((64, 64), 1)
    order_tails = onehot(o64 == ((i64 >> 1) & 3) * 16 + (i64 >> 3) * 2 + (i64 & 1))
    tail = dot(order_tails, tails).astype(BF16)
    X[64:80, 0:HALF] = tail[0:16]
    X[64:80, HALF:] = tail[16:32]
    G[64:80, 0:HALF] = tail[32:48]
    G[64:80, HALF:] = tail[48:64]

    for c in range(NX):
        at = column[c] * 2 + 1 - core
        for i in range(2):
            w_in(i, at, twin)

    last = ((1,), (1,))
    hidden, width = NX * 2 * 80, 2 * HALF
    pre = dot(W1[...].reshape(hidden, width), X[...], last)
    dh = dot(W2[...].reshape(hidden, width), G[...], last)
    k0 = 0.7978845608028654
    sq = pre * pre
    t = jnp.tanh(k0 * (pre + 0.044715 * (sq * pre)))
    cdf = 0.5 * (1.0 + t)
    act = (pre * cdf).astype(BF16)
    slope = cdf + pre * (0.5 * (1.0 - t * t)) * (k0 * (1.0 + 3 * 0.044715 * sq))
    dpre32 = dh * slope
    dpre = dpre32.astype(BF16)
    dx[...] = dot(dpre32.T.astype(BF16), W1[...].reshape(hidden, width)).astype(BF16)

    q_row, q_col = iota((24, 80), 0), iota((24, 80), 1)

    def group_rows(half, yy):
        q_slot = q_row - 10 * half
        inside = (q_slot >= 0) & (q_slot < 10)
        source = jnp.where(q_slot < 8, yy * 8 + q_slot, 56 + yy * 2 + q_slot)
        return onehot(inside & (q_col == source))

    def piece(d):
        yy = number(d)
        return dot(group_rows(0, yy), dx[:, :HALF]) + dot(group_rows(1, yy), dx[:, HALF:])

    for d in groups_first:
        csend[d - 1] = piece(d).astype(BF16)
        send(csend.at[d - 1], crecv.at[d - 1], c_send.at[d - 1], c_recv.at[d - 1], group_peer[d])
    total = piece(0)

    for i, (left, right) in enumerate(((dpre, X), (act, G))):
        full = dot(left, right[...])
        for k in range(2 * NX):
            gtwin[i, k] = full[k * 80:(k + 1) * 80]
    for c in (3, 2, 1, 0):
        at = column[c] * 2 + 1 - core
        for i in range(2):
            send(gtwin.at[i, at], gfrom.at[i, column[c]], t_send.at[i, c], t_recv.at[i, column[c]], twin)

    def g_go(c, i):
        arrived(gfrom.at[i, column[c]], t_recv.at[i, column[c]], t_send.at[i, c], twin)
        both = gtwin[i, column[c] * 2 + core] + gfrom[i, column[c]]
        gsend[c - 1, i] = both.astype(BF16)
        send(gsend.at[c - 1, i], grecv.at[c - 1, i], g_send.at[c - 1, i], g_recv.at[c - 1, i], chip_peer[c])

    g_go(1, 0)
    g_go(2, 0)

    r64 = iota((128, 64), 0)
    gather = onehot(iota((128, 64), 1) == (r64 >> 3) * 4 + (r64 & 3))
    v_row = dot(gather, v8.astype(BF16), last)[:, 0:1]
    t_row, t_col = iota((128, 24), 0), iota((128, 24), 1)
    t_half = (t_col >= 10).astype(jnp.int32)
    t_slot = jnp.where(t_col < 20, t_col - 10 * t_half, 50).astype(F32)
    back = onehot((v_row == t_slot) & (((t_row >> 2) & 1) == t_half))

    for d in range(1, NY):
        arrived(crecv.at[d - 1], c_recv.at[d - 1], c_send.at[d - 1], group_peer[seen[d]])
        total = total + crecv[d - 1].astype(F32)
    spread_rows = dot(back, total.astype(BF16))
    dsend[...] = spread_rows.reshape(NE, 8, HALF).astype(BF16)
    for d in (8, 12, 4, 9, 7, 10, 6, 11, 5, 13, 3, 14, 2, 15, 1):
        pltpu.make_async_remote_copy(
            src_ref=dsend.at[(e + d) % NE], dst_ref=drecv.at[d - 1],
            send_sem=d_send, recv_sem=d_recv, device_id=e_peer[d], device_id_type=MESH,
        ).start()

    g_go(3, 0)
    g_go(3, 1)
    g_go(1, 1)
    g_go(2, 1)
    for i in range(2):
        arrived(gfrom.at[i, home], t_recv.at[i, home], t_send.at[i, 0], twin)
    landed = pltpu.make_async_remote_copy(
        src_ref=drecv, dst_ref=drecv, send_sem=d_send, recv_sem=d_recv,
        device_id=e_peer[1], device_id_type=MESH,
    )
    landed.wait_recv()
    res = dsend[e].astype(F32)
    for d in range(1, NE):
        res = res + drecv[d - 1].astype(F32)
    out_tok[:, :HALF] = res[0:4].astype(BF16)
    out_tok[:, HALF:] = res[4:8].astype(BF16)
    for c in (1, 2, 3):
        for i in range(2):
            arrived(grecv.at[c - 1, i], g_recv.at[c - 1, i], g_send.at[c - 1, i], chip_peer[c])
    for i, out in ((0, out_in), (1, out_out)):
        res = gtwin[i, me] + gfrom[i, home]
        for c in range(1, NX):
            res = res + grecv[c - 1, i].astype(F32)
        out[...] = res
    landed.wait_send()
    for copy in started:
        copy.wait_send()


def local(tokens, upstream, experts, gates, w_in, w_out):
    vmem = pl.BlockSpec(memory_space=pltpu.VMEM)
    dma = pltpu.SemaphoreType.DMA
    width = 2 * HALF
    out_tok, out_in, out_out = pl.pallas_call(
        kernel,
        out_shape=(
            jax.ShapeDtypeStruct((4, width), BF16),
            jax.ShapeDtypeStruct((80, width), F32),
            jax.ShapeDtypeStruct((80, width), F32),
        ),
        in_specs=[pl.BlockSpec(memory_space=pltpu.HBM)] * 6,
        out_specs=(vmem, vmem, vmem),
        scratch_shapes=[
            pltpu.VMEM((4, width), BF16),
            pltpu.VMEM((4, width), BF16),
            pltpu.VMEM((2, 64), jnp.int32),
            pltpu.VMEM((2, 64), F32),
            pltpu.VMEM((NE, 16, HALF), BF16),
            pltpu.VMEM((NY, 40, HALF), BF16),
            pltpu.VMEM((80, width), BF16),
            pltpu.VMEM((80, width), BF16),
            pltpu.VMEM((2 * NX, 80, width), BF16),
            pltpu.VMEM((2 * NX, 80, width), BF16),
            pltpu.VMEM((80, width), BF16),
            pltpu.VMEM((NY - 1, 24, HALF), BF16),
            pltpu.VMEM((NY - 1, 24, HALF), BF16),
            pltpu.VMEM((NE, 8, HALF), BF16),
            pltpu.VMEM((NE - 1, 8, HALF), BF16),
            pltpu.VMEM((2, 2 * NX, 80, width), F32),
            pltpu.VMEM((2, NX, 80, width), F32),
            pltpu.VMEM((NX - 1, 2, 80, width), BF16),
            pltpu.VMEM((NX - 1, 2, 80, width), BF16),
            dma((6,)), dma((NE,)), dma((NE,)), dma((2, 7)), dma((2, 2 * NX)), dma((NY,)), dma((NY,)),
            dma((NY - 1,)), dma((NY - 1,)), dma, dma, dma((2, NX)), dma((2, NX)),
            dma((NX - 1, 2)), dma((NX - 1, 2)),
        ],
        compiler_params=pltpu.CompilerParams(
            collective_id=0, has_side_effects=True, vmem_limit_bytes=48 * 1024 * 1024
        ),
        cost_estimate=pl.CostEstimate(flops=700_000_000, bytes_accessed=2_000_000, transcendentals=51200),
        name="moe_backward",
    )(tokens, upstream, experts.T, gates.T, w_in[0].T, w_out[0])
    return out_tok, out_in.T[None], out_out[None]


def solution(mesh):
    in_specs = (
        P(("replica", "expert"), None),
        P(("replica", "expert"), None),
        P("replica", None),
        P("replica", None),
        P("expert", None, "replica"),
        P("expert", "replica", None),
    )
    out_specs = (
        P(("replica", "expert"), None),
        P("expert", None, "replica"),
        P("expert", "replica", None),
    )
    return jax.shard_map(local, mesh=mesh, in_specs=in_specs, out_specs=out_specs, check_vma=False)
```

time: 95.9 us -> 88.2 us (0.920)
  the two profiles are of different devices: /device:TPU:16 before, /device:TPU:1 now
where the time goes in v2:
time: 88.2 us; the launch traced here: 87.8 us
  Pallas kernels  81.1 us (92%)
  local copies, waits for them, and re-layouts  6.05 us (7%)
    pallas_call x1, Pallas kernels, local(): pl.pallas_call(kernel, out_shape=(jax.ShapeDtypeStruct((4, width), BF16),...  81.1 us
    unnamed x15, local copies, waits for them, and re-layouts  6.05 us

profile of v2, /device:TPU:1, one launch (start us, length us, event | category | flops | bytes accessed | tf_op | source)
XLA Modules:
  0.0 87.8 jit_solution(11157747173491203253)
XLA Ops:
  0.6 0.0 copy-start.5
  0.6 0.0 copy-start.4
  0.7 0.7 copy-done.5
  1.3 0.0 copy-done.4
  1.3 0.0 copy-start
  1.3 0.9 %copy-done = bf16[1,1280,80]{1,2,0:T(8,128)(2,1)S(1)} copy-done((bf16[1,1280,80]{1,2,0:T(8,128)(2,1)S(1)}, bf16[1,1280,80]{1,2,0:T(8,128)(2,1)}, u32[]{:S(2)}) %copy-start) | copy-done | bytes 204824
  2.3 0.0 copy-start.1
  2.3 0.9 %copy-done.1 = bf16[1,80,1280]{2,1,0:T(8,128)(2,1)S(1)} copy-done((bf16[1,80,1280]{2,1,0:T(8,128)(2,1)S(1)}, bf16[1,80,1280]{2,1,0:T(8,128)(2,1)}, u32[]{:S(2)}) %copy-start.1) | copy-done | bytes 204824
  3.2 0.0 copy-start.2
  3.2 0.7 copy-done.2
  3.9 0.0 copy-start.3
  3.9 0.7 copy-done.3
  4.6 81.1 %moe_backward.1 = (bf16[4,1280]{1,0:T(4,128)(2,1)S(1)}, f32[80,1280]{1,0:T(8,128)S(1)}, f32[80,1280]{1,0:T(8,128)S(1)}) custom-call(bf16[4,1280]{1,0:T(4,128)(2,1)S(1)} %copy-done.2, bf16[4,1280]{1,0:T(4,128)(2,1)S(1)} %copy-done.3, s32[2,64]{1,0:T(2,128)S(1)} %bitcast.14, f32[2,64]{1,0:T(2,128)S(1)} %bitcast.15, bf16[80,1280]{1,0:T(8,128)(2,1)S(1)} %bitcast.12, ...), custom_call_target="tpu_custom_call" | custom-call | flops 700000000 | bytes 2000000 | tf_op jit(solution)/shard_map/moe_backward/pallas_call | solution.py:309
  85.7 0.6 copy.12
  86.3 0.8 copy.13
  87.1 0.8 copy.14
Async XLA Ops:
  0.6 0.7 copy-start.5
  0.6 0.7 copy-start.4
  1.3 0.9 %copy-start = (bf16[1,1280,80]{1,2,0:T(8,128)(2,1)S(1)}, bf16[1,1280,80]{1,2,0:T(8,128)(2,1)}, u32[]{:S(2)}) copy-start(bf16[1,1280,80]{1,2,0:T(8,128)(2,1)} %param.10) | copy-start | bytes 614404
  2.3 0.9 %copy-start.1 = (bf16[1,80,1280]{2,1,0:T(8,128)(2,1)S(1)}, bf16[1,80,1280]{2,1,0:T(8,128)(2,1)}, u32[]{:S(2)}) copy-start(bf16[1,80,1280]{2,1,0:T(8,128)(2,1)} %param.11) | copy-start | bytes 614404
  3.2 0.7 copy-start.2
  3.9 0.7 copy-start.3

commit v3 on v2

--- a/solution.py
+++ b/solution.py
@@ -131,6 +131,8 @@
     w_go(0, me, 2, chip_peer[2])
     w_go(0, me, 0, twin)
     w_go(1, me, 0, twin)
+    w_go(1, me, 1, chip_peer[1])
+    w_go(1, me, 2, chip_peer[2])
 
     loads[2].wait()
     loads[3].wait()
@@ -157,8 +159,17 @@
     arrived(abuf.at[pe], a_recv.at[pe], a_send.at[0], mirror)
     for d in far_first:
         send(abuf.at[pe], abuf.at[pe], a_send.at[NZ + d], a_recv.at[pe], z_peer[d])
-    w_go(1, me, 1, chip_peer[1])
-    w_go(1, me, 2, chip_peer[2])
+    ats = [column[c] * 2 + core for c in range(4)]
+    w_in(0, ats[1], chip_peer[1])
+    w_go(0, ats[1], 3, chip_peer[2])
+    w_go(0, ats[1], 4, twin)
+    w_in(0, ats[2], chip_peer[2])
+    w_go(0, ats[2], 5, twin)
+    w_in(1, ats[2], chip_peer[2])
+    w_go(1, ats[2], 3, chip_peer[1])
+    w_go(1, ats[2], 4, twin)
+    w_in(1, ats[1], chip_peer[1])
+    w_go(1, ats[1], 5, twin)
     for h in range(2):
         for d in range(1, NZ):
             s = ((xh + h) % 2) * NZ + (z + d) % NZ
@@ -169,22 +180,10 @@
     for d in groups_first:
         send(bbuf.at[this], bbuf.at[this], b_send.at[d], b_recv.at[this], group_peer[d])
 
-    ats = [column[c] * 2 + core for c in range(4)]
-    w_in(0, ats[1], chip_peer[1])
-    w_go(0, ats[1], 3, chip_peer[2])
-    w_in(1, ats[2], chip_peer[2])
-    w_go(1, ats[2], 3, chip_peer[1])
-    w_go(0, ats[1], 4, twin)
-    w_go(1, ats[2], 4, twin)
-    w_in(0, ats[2], chip_peer[2])
-    w_go(0, ats[2], 5, twin)
-    w_in(1, ats[1], chip_peer[1])
-    w_go(1, ats[1], 5, twin)
     w_in(0, ats[3], chip_peer[2])
     w_go(0, ats[3], 6, twin)
     w_in(1, ats[3], chip_peer[1])
     w_go(1, ats[3], 6, twin)
-
     for d in range(1, NY):
         yy = number(d)
         arrived(bbuf.at[yy], b_recv.at[yy], b_send.at[0], group_peer[d])
@@ -240,19 +239,25 @@
         full = dot(left, right[...])
         for k in range(2 * NX):
             gtwin[i, k] = full[k * 80:(k + 1) * 80]
-    for c in (3, 2, 1, 0):
+    for c in (3, 1, 2, 0):
         at = column[c] * 2 + 1 - core
         for i in range(2):
             send(gtwin.at[i, at], gfrom.at[i, column[c]], t_send.at[i, c], t_recv.at[i, column[c]], twin)
 
-    def g_go(c, i):
+    def both_cores(c, i):
         arrived(gfrom.at[i, column[c]], t_recv.at[i, column[c]], t_send.at[i, c], twin)
-        both = gtwin[i, column[c] * 2 + core] + gfrom[i, column[c]]
-        gsend[c - 1, i] = both.astype(BF16)
-        send(gsend.at[c - 1, i], grecv.at[c - 1, i], g_send.at[c - 1, i], g_recv.at[c - 1, i], chip_peer[c])
-
-    g_go(1, 0)
-    g_go(2, 0)
+        return gtwin[i, column[c] * 2 + core] + gfrom[i, column[c]]
+
+    def g_go(c, i, value, peer):
+        gsend[c - 1, i] = value.astype(BF16)
+        send(gsend.at[c - 1, i], grecv.at[c - 1, i], g_send.at[c - 1, i], g_recv.at[c - 1, i], peer)
+
+    def g_in(c, i, peer):
+        arrived(grecv.at[c - 1, i], g_recv.at[c - 1, i], g_send.at[c - 1, i], peer)
+        return grecv[c - 1, i].astype(F32)
+
+    g_go(3, 0, both_cores(3, 0), chip_peer[2])
+    g_go(3, 1, both_cores(3, 1), chip_peer[2])
 
     r64 = iota((128, 64), 0)
     gather = onehot(iota((128, 64), 1) == (r64 >> 3) * 4 + (r64 & 3))
@@ -273,12 +278,9 @@
             send_sem=d_send, recv_sem=d_recv, device_id=e_peer[d], device_id_type=MESH,
         ).start()
 
-    g_go(3, 0)
-    g_go(3, 1)
-    g_go(1, 1)
-    g_go(2, 1)
     for i in range(2):
-        arrived(gfrom.at[i, home], t_recv.at[i, home], t_send.at[i, 0], twin)
+        g_go(1, i, both_cores(1, i) + g_in(3, i, chip_peer[2]), chip_peer[1])
+        g_go(2, i, both_cores(2, i), chip_peer[2])
     landed = pltpu.make_async_remote_copy(
         src_ref=drecv, dst_ref=drecv, send_sem=d_send, recv_sem=d_recv,
         device_id=e_peer[1], device_id_type=MESH,
@@ -289,14 +291,8 @@
         res = res + drecv[d - 1].astype(F32)
     out_tok[:, :HALF] = res[0:4].astype(BF16)
     out_tok[:, HALF:] = res[4:8].astype(BF16)
-    for c in (1, 2, 3):
-        for i in range(2):
-            arrived(grecv.at[c - 1, i], g_recv.at[c - 1, i], g_send.at[c - 1, i], chip_peer[c])
     for i, out in ((0, out_in), (1, out_out)):
-        res = gtwin[i, me] + gfrom[i, home]
-        for c in range(1, NX):
-            res = res + grecv[c - 1, i].astype(F32)
-        out[...] = res
+        out[...] = both_cores(0, i) + g_in(1, i, chip_peer[1]) + g_in(2, i, chip_peer[2])
     landed.wait_send()
     for copy in started:
         copy.wait_send()
@@ -340,7 +336,7 @@
             dma((NX - 1, 2)), dma((NX - 1, 2)),
         ],
         compiler_params=pltpu.CompilerParams(
-            collective_id=0, has_side_effects=True, vmem_limit_bytes=48 * 1024 * 1024
+            collective_id=0, has_side_effects=True, vmem_limit_bytes=62 * 1024 * 1024
         ),
         cost_estimate=pl.CostEstimate(flops=700_000_000, bytes_accessed=2_000_000, transcendentals=51200),
         name="moe_backward",

time: 88.2 us -> 81.8 us (0.927)
  Pallas kernels: 81.1 us -> 77 us
  local copies, waits for them, and re-layouts: 6.05 us -> 3.89 us
    pallas_call x1, Pallas kernels: 81.1 us -> 77 us  [local(): pl.pallas_call(kernel, out_shape=(jax.ShapeDtypeStruct((4, width), BF16),...]
    unnamed x15 -> x5, local copies, waits for them, and re-layouts: 6.05 us -> 3.89 us
where the time goes in v3:
time: 81.8 us; the launch traced here: 81.5 us
  Pallas kernels  77 us (94%)
  local copies, waits for them, and re-layouts  3.89 us (5%)
    pallas_call x1, Pallas kernels, local(): pl.pallas_call(kernel, out_shape=(jax.ShapeDtypeStruct((4, width), BF16),...  77 us
    unnamed x5, local copies, waits for them, and re-layouts  3.89 us

profile of v3, /device:TPU:1, one launch (start us, length us, event | category | flops | bytes accessed | tf_op | source)
XLA Modules:
  0.0 81.5 jit_solution(15806151372072693650)
XLA Ops:
  0.6 77.0 %moe_backward.1 = (bf16[4,1280]{1,0:T(4,128)(2,1)}, f32[80,1280]{1,0:T(8,128)}, f32[80,1280]{1,0:T(8,128)}) custom-call(bf16[4,1280]{1,0:T(4,128)(2,1)} %tok_hbm.1, bf16[4,1280]{1,0:T(4,128)(2,1)} %up_hbm.1, s32[2,64]{1,0:T(2,128)} %bitcast.14, f32[2,64]{1,0:T(2,128)} %bitcast.15, bf16[80,1280]{1,0:T(8,128)(2,1)} %bitcast.12, bf16[80,1280]{1,0:T(8,128)(2,1)} %bitcast.13), custom_call_target="tpu_custom_call" | custom-call | flops 700000000 | bytes 2000000 | tf_op jit(solution)/shard_map/moe_backward/pallas_call | solution.py:305
  77.6 1.3 %copy.12 = bf16[4,1280]{1,0:T(4,128)(2,1)} copy(bf16[4,1280]{1,0:T(4,128)(2,1)} %get-tuple-element.12) | data formatting | bytes 20480
  78.9 0.0 copy-start
  78.9 1.8 %copy.13 = f32[1,1280,80]{1,2,0:T(8,128)} copy(f32[1,1280,80]{1,2,0:T(8,128)} %bitcast.11) | data formatting | bytes 819200
  80.8 0.0 copy-done
  80.8 0.8 copy.14
Async XLA Ops:
  78.9 1.8 %copy-start = (f32[80,1280]{1,0:T(8,128)S(1)}, f32[80,1280]{1,0:T(8,128)}, u32[]{:S(2)}) copy-start(f32[80,1280]{1,0:T(8,128)} %get-tuple-element.8) | copy-start | bytes 1228804

commit v4 on v3

--- a/solution.py
+++ b/solution.py
@@ -239,9 +239,8 @@
         full = dot(left, right[...])
         for k in range(2 * NX):
             gtwin[i, k] = full[k * 80:(k + 1) * 80]
-    for c in (3, 1, 2, 0):
-        at = column[c] * 2 + 1 - core
-        for i in range(2):
+        for c in (3, 2, 1, 0):
+            at = column[c] * 2 + 1 - core
             send(gtwin.at[i, at], gfrom.at[i, column[c]], t_send.at[i, c], t_recv.at[i, column[c]], twin)
 
     def both_cores(c, i):
@@ -258,6 +257,8 @@
 
     g_go(3, 0, both_cores(3, 0), chip_peer[2])
     g_go(3, 1, both_cores(3, 1), chip_peer[2])
+    g_go(2, 0, both_cores(2, 0), chip_peer[2])
+    g_go(2, 1, both_cores(2, 1), chip_peer[2])
 
     r64 = iota((128, 64), 0)
     gather = onehot(iota((128, 64), 1) == (r64 >> 3) * 4 + (r64 & 3))
@@ -280,7 +281,6 @@
 
     for i in range(2):
         g_go(1, i, both_cores(1, i) + g_in(3, i, chip_peer[2]), chip_peer[1])
-        g_go(2, i, both_cores(2, i), chip_peer[2])
     landed = pltpu.make_async_remote_copy(
         src_ref=drecv, dst_ref=drecv, send_sem=d_send, recv_sem=d_recv,
         device_id=e_peer[1], device_id_type=MESH,
@@ -300,14 +300,18 @@
 
 def local(tokens, upstream, experts, gates, w_in, w_out):
     vmem = pl.BlockSpec(memory_space=pltpu.VMEM)
+
+    def hbm(a):
+        return pltpu.with_memory_space_constraint(a, pltpu.HBM)
+
     dma = pltpu.SemaphoreType.DMA
     width = 2 * HALF
     out_tok, out_in, out_out = pl.pallas_call(
         kernel,
         out_shape=(
-            jax.ShapeDtypeStruct((4, width), BF16),
-            jax.ShapeDtypeStruct((80, width), F32),
-            jax.ShapeDtypeStruct((80, width), F32),
+            pltpu.VMEM((4, width), BF16),
+            pltpu.VMEM((80, width), F32),
+            pltpu.VMEM((80, width), F32),
         ),
         in_specs=[pl.BlockSpec(memory_space=pltpu.HBM)] * 6,
         out_specs=(vmem, vmem, vmem),
@@ -336,11 +340,11 @@
             dma((NX - 1, 2)), dma((NX - 1, 2)),
         ],
         compiler_params=pltpu.CompilerParams(
-            collective_id=0, has_side_effects=True, vmem_limit_bytes=62 * 1024 * 1024
+            collective_id=0, has_side_effects=True, vmem_limit_bytes=56 * 1024 * 1024
         ),
         cost_estimate=pl.CostEstimate(flops=700_000_000, bytes_accessed=2_000_000, transcendentals=51200),
         name="moe_backward",
-    )(tokens, upstream, experts.T, gates.T, w_in[0].T, w_out[0])
+    )(*(hbm(a) for a in (tokens, upstream, experts.T, gates.T, w_in[0].T, w_out[0])))
     return out_tok, out_in.T[None], out_out[None]
 
 

time: 81.8 us -> 79.1 us (0.967)
  local copies, waits for them, and re-layouts: 3.89 us -> 2.1 us
    unnamed x5 -> x3, local copies, waits for them, and re-layouts: 3.89 us -> 2.1 us
where the time goes in v4:
time: 79.1 us; the launch traced here: 79 us
  Pallas kernels  76.2 us (96%)
  local copies, waits for them, and re-layouts  2.1 us (3%)
    pallas_call x1, Pallas kernels, local(): pl.pallas_call(kernel, out_shape=(pltpu.VMEM((4, width), BF16), pltpu.VME...  76.2 us
    unnamed x3, local copies, waits for them, and re-layouts  2.1 us

profile of v4, /device:TPU:1, one launch (start us, length us, event | category | flops | bytes accessed | tf_op | source)
XLA Modules:
  0.0 79.0 jit_solution(10820098895782838829)
XLA Ops:
  0.6 76.2 %moe_backward.1 = (bf16[4,1280]{1,0:T(4,128)(2,1)S(1)}, f32[80,1280]{1,0:T(8,128)S(1)}, f32[80,1280]{1,0:T(8,128)S(1)}) custom-call(bf16[4,1280]{1,0:T(4,128)(2,1)} %tok_hbm.1, bf16[4,1280]{1,0:T(4,128)(2,1)} %up_hbm.1, s32[2,64]{1,0:T(2,128)} %bitcast.14, f32[2,64]{1,0:T(2,128)} %bitcast.15, bf16[80,1280]{1,0:T(8,128)(2,1)} %bitcast.12, ...), custom_call_target="tpu_custom_call" | custom-call | flops 700000000 | bytes 2000000 | tf_op jit(solution)/shard_map/moe_backward/pallas_call | solution.py:309
  76.8 0.6 copy.12
  77.5 0.8 copy.13
  78.2 0.8 copy.14

commit v5 on v4

--- a/solution.py
+++ b/solution.py
@@ -235,17 +235,21 @@
         send(csend.at[d - 1], crecv.at[d - 1], c_send.at[d - 1], c_recv.at[d - 1], group_peer[d])
     total = piece(0)
 
+    def to_twin(c, i):
+        at = column[c] * 2 + 1 - core
+        send(gtwin.at[i, at], gfrom.at[i, column[c]], t_send.at[i, c], t_recv.at[i, column[c]], twin)
+
     for i, (left, right) in enumerate(((dpre, X), (act, G))):
         full = dot(left, right[...])
         for k in range(2 * NX):
-            gtwin[i, k] = full[k * 80:(k + 1) * 80]
-        for c in (3, 2, 1, 0):
-            at = column[c] * 2 + 1 - core
-            send(gtwin.at[i, at], gfrom.at[i, column[c]], t_send.at[i, c], t_recv.at[i, column[c]], twin)
+            gtwin[i, k] = full[k * 80:(k + 1) * 80].astype(BF16)
+        to_twin(3, i)
+    to_twin(2, 0)
+    to_twin(2, 1)
 
     def both_cores(c, i):
         arrived(gfrom.at[i, column[c]], t_recv.at[i, column[c]], t_send.at[i, c], twin)
-        return gtwin[i, column[c] * 2 + core] + gfrom[i, column[c]]
+        return gtwin[i, column[c] * 2 + core].astype(F32) + gfrom[i, column[c]].astype(F32)
 
     def g_go(c, i, value, peer):
         gsend[c - 1, i] = value.astype(BF16)
@@ -257,6 +261,9 @@
 
     g_go(3, 0, both_cores(3, 0), chip_peer[2])
     g_go(3, 1, both_cores(3, 1), chip_peer[2])
+    for c in (1, 0):
+        for i in range(2):
+            to_twin(c, i)
     g_go(2, 0, both_cores(2, 0), chip_peer[2])
     g_go(2, 1, both_cores(2, 1), chip_peer[2])
 
@@ -331,8 +338,8 @@
             pltpu.VMEM((NY - 1, 24, HALF), BF16),
             pltpu.VMEM((NE, 8, HALF), BF16),
             pltpu.VMEM((NE - 1, 8, HALF), BF16),
-            pltpu.VMEM((2, 2 * NX, 80, width), F32),
-            pltpu.VMEM((2, NX, 80, width), F32),
+            pltpu.VMEM((2, 2 * NX, 80, width), BF16),
+            pltpu.VMEM((2, NX, 80, width), BF16),
             pltpu.VMEM((NX - 1, 2, 80, width), BF16),
             pltpu.VMEM((NX - 1, 2, 80, width), BF16),
             dma((6,)), dma((NE,)), dma((NE,)), dma((2, 7)), dma((2, 2 * NX)), dma((NY,)), dma((NY,)),

time: 79.1 us -> 79.1 us (level)
  no operation moved by 1% of the time
where the time goes in v5:
time: 79.1 us; the launch traced here: 78.9 us
  Pallas kernels  76.2 us (96%)
  local copies, waits for them, and re-layouts  2.1 us (3%)
    pallas_call x1, Pallas kernels, local(): pl.pallas_call(kernel, out_shape=(pltpu.VMEM((4, width), BF16), pltpu.VME...  76.2 us
    unnamed x3, local copies, waits for them, and re-layouts  2.1 us

profile of v5, /device:TPU:1, one launch (start us, length us, event | category | flops | bytes accessed | tf_op | source)
XLA Modules:
  0.0 78.9 jit_solution(12907701576218045923)
XLA Ops:
  0.6 76.2 %moe_backward.1 = (bf16[4,1280]{1,0:T(4,128)(2,1)S(1)}, f32[80,1280]{1,0:T(8,128)S(1)}, f32[80,1280]{1,0:T(8,128)S(1)}) custom-call(bf16[4,1280]{1,0:T(4,128)(2,1)} %tok_hbm.1, bf16[4,1280]{1,0:T(4,128)(2,1)} %up_hbm.1, s32[2,64]{1,0:T(2,128)} %bitcast.14, f32[2,64]{1,0:T(2,128)} %bitcast.15, bf16[80,1280]{1,0:T(8,128)(2,1)} %bitcast.12, ...), custom_call_target="tpu_custom_call" | custom-call | flops 700000000 | bytes 2000000 | tf_op jit(solution)/shard_map/moe_backward/pallas_call | solution.py:316
  76.8 0.6 copy.12
  77.4 0.8 copy.13
  78.1 0.8 copy.14
